TPU v7x, 32 devices: a whole 2x2x4 slice. The times are simulated.
32 devices in a mesh: dom: 8 (over y, x, core), near: 4 (over z).
Axes of the slice: x: 2, y: 2, z: 4, core: 2. Of those that a mesh axis runs over, the one named last changes fastest.
Arguments:
- start_block: float32 [32768, 128], P(('dom', 'near')), may hold values from -6 to 6
- near_tiles: float32 [1536, 128, 128], P(('dom', 'near')), may hold values from -0.09375 to 0.09375
- near_src: int32 [1536], P(('dom', 'near')), may hold values from 0 to 31, as said below
- near_mask: int32 [1536], P(('dom', 'near')), may hold values 0 or 1
- far_tiles: float32 [256, 128, 128], P(('dom', 'near')), may hold values from -0.09375 to 0.09375
- far_src: int32 [256], P(('dom', 'near')), may hold values from 0 to 7
- far_mask: int32 [256], P(('dom', 'near')), may hold values 0 or 1
- bound_count: int32 [32], P(('dom', 'near')), may hold values from 1 to 128
Outputs:
- encodings: float32 [32768, 128], P(('dom', 'near'))
- rayleigh: float32 [128, 128], replicated
Inputs may be any that keep to these rules, and one draw needn't show every extreme that they name: `near_src`: each partition holds 48 consecutive slots; the slot at position j among them (j from 0) lies in tile row j // 6; the first slot of each tile row reads the partition's own tile of that row; every source tile from another partition of the group is one of that partition's first 4 tiles.
All inputs are finite; a program needn't handle non-finite values. No bound on the sum of `near_mask` or of `far_mask` on one device may be relied on, other than what follows from the above.
Results may differ from a plain program's by a relative error of at most 0.0003.
Values sent between devices are 32-bit elements; how exact they have to be, the bound alone decides.
A program may use at most 64 MiB of HBM per device.

v0:
```python
from functools import partial

import jax
import jax.numpy as jnp
from jax import lax
from jax.sharding import PartitionSpec as P

NPER = 6
ITERS = 2
DEG = 3


LOWER_EDGE = 0.6
UPPER_EDGE = 2.0


def apply_operator(
    block, near_tiles, near_src, near_mask, far_tiles, far_src, far_mask, bound_count
):
    tile_rows = near_tiles.shape[1]
    width = block.shape[1]
    tiles_dev = block.shape[0] // tile_rows
    group_size = lax.axis_size("near")
    gathered = lax.all_gather(block, "near", axis=0, tiled=True)
    picked = gathered.reshape(group_size * tiles_dev, tile_rows, width)[near_src]
    products = jnp.einsum("sij,sjk->sik", near_tiles, picked, precision=lax.Precision.HIGHEST)
    products = products * near_mask.astype(jnp.float32)[:, None, None]
    near_sum = products.reshape(tiles_dev, NPER, tile_rows, width).sum(axis=1)
    limit = (jnp.arange(tile_rows) < bound_count[0]).astype(jnp.float32)
    edge_tile = block[:tile_rows] * limit[:, None]
    edges = lax.all_gather(edge_tile, "dom", axis=0, tiled=True).reshape(
        lax.axis_size("dom"), tile_rows, width
    )
    far_pick = edges[far_src]
    far_sum = jnp.einsum("sij,sjk->sik", far_tiles, far_pick, precision=lax.Precision.HIGHEST)
    far_sum = far_sum * far_mask.astype(jnp.float32)[:, None, None]
    return block - (near_sum + far_sum).reshape(block.shape)


def chebyshev(current, image, operator):
    center = (UPPER_EDGE + LOWER_EDGE) / 2.0
    half = (UPPER_EDGE - LOWER_EDGE) / 2.0
    previous = current
    present = (image - center * current) / half
    for degree in range(DEG - 1):
        following = 2.0 * (operator(present) - center * present) / half - previous
        previous, present = (present, following)
    return present


def inner(left, right):
    return jnp.dot(
        left.T, right, precision=lax.Precision.HIGHEST, preferred_element_type=jnp.float32
    )


def times_inverse(block, lower_inv):
    return jnp.dot(
        block, lower_inv.T, precision=lax.Precision.HIGHEST, preferred_element_type=jnp.float32
    )


def inverse_factor(gram):
    lower = jnp.linalg.cholesky(gram)
    return jax.scipy.linalg.solve_triangular(
        lower, jnp.eye(gram.shape[0], dtype=jnp.float32), lower=True
    )


def local(start_block, near_tiles, near_src, near_mask, far_tiles, far_src, far_mask, bound_count):
    operator = partial(
        apply_operator,
        near_tiles=near_tiles,
        near_src=near_src,
        near_mask=near_mask,
        far_tiles=far_tiles,
        far_src=far_src,
        far_mask=far_mask,
        bound_count=bound_count,
    )
    nodes_all = start_block.shape[0] * lax.axis_size("dom") * lax.axis_size("near")
    current = start_block
    image = operator(current)
    cross = None
    lower_inv = None
    for iteration in range(ITERS):
        filtered = chebyshev(current, image, operator)
        filtered_image = operator(filtered)
        gram, cross = lax.psum(
            (inner(filtered, filtered), inner(filtered, filtered_image)), ("dom", "near")
        )
        gram = gram / nodes_all
        cross = cross / nodes_all
        lower_inv = inverse_factor(gram)
        current = times_inverse(filtered, lower_inv)
        image = times_inverse(filtered_image, lower_inv)
    rayleigh = jnp.dot(
        jnp.dot(
            lower_inv, cross, precision=lax.Precision.HIGHEST, preferred_element_type=jnp.float32
        ),
        lower_inv.T,
        precision=lax.Precision.HIGHEST,
        preferred_element_type=jnp.float32,
    )
    return (current, rayleigh)


def solution(mesh):
    return jax.shard_map(
        local,
        mesh=mesh,
        in_specs=(
            P(("dom", "near"), None),
            P(("dom", "near"), None, None),
            P(("dom", "near")),
            P(("dom", "near")),
            P(("dom", "near"), None, None),
            P(("dom", "near")),
            P(("dom", "near")),
            P(("dom", "near")),
        ),
        out_specs=(P(("dom", "near"), None), P()),
        check_vma=False,
    )
```

profile of v0, /device:TPU:0, one launch (start us, length us, event | category | flops | bytes accessed | tf_op | source)
XLA Modules:
  0.0 760.7 jit_solution(17351797407002268105)
XLA Ops:
  11.7 12.4 %all_gather.43 = f32[1024,128]{1,0:T(8,128)} all-gather(f32[128,128]{1,0:T(8,128)S(1)} %slice_multiply_fusion.6), channel_id=1, replica_groups=mesh['dom'=8,'near'=4] {'dom'}, dimensions={0}, use_global_device_ids=true | all-gather | bytes 589824 | tf_op jit(solution)/shard_map/all_gather | solution.py:31
  24.0 2.4 gather_fusion.1
  27.1 31.1 %all-gather.8.cloned.1.call-done = f32[4096,128]{1,0:T(8,128)} async-done(((f32[1024,128]{1,0:T(8,128)}), f32[4096,128]{1,0:T(8,128)}) %all-gather.8.cloned.1.call-update) | async-done | bytes 2097168 | tf_op jit(solution)/shard_map/all_gather | solution.py:24
  58.3 4.0 gather_fusion
  62.3 8.1 %convolution_multiply_fusion.6 = f32[48,128,128]{2,1,0:T(8,128)} fusion(f32[48,128,128]{2,1,0:T(8,128)} %gather_fusion, f32[48,128,128]{2,1,0:T(8,128)S(1)} %copy-done, f32[48]{0:T(128)S(1)} %convert_element_type.14), kind=kOutput, calls=%fused_computation.20 | convolution fusion | flops 1208745984 | bytes 9437376 | tf_op jit(solution)/shard_map/sij,sjk->sik/dot_general | solution.py:26
  70.4 2.9 reduce_sum.63
  73.3 2.0 copy.26
  81.0 10.8 %all_gather.45 = f32[1024,128]{1,0:T(8,128)} all-gather(f32[128,128]{1,0:T(8,128)S(1)} %slice_multiply_fusion.5), channel_id=1, replica_groups=mesh['dom'=8,'near'=4] {'dom'}, dimensions={0}, use_global_device_ids=true | all-gather | bytes 589824 | tf_op jit(solution)/shard_map/all_gather | solution.py:31
  91.8 2.4 gather_fusion.3
  94.3 30.6 %all-gather.10.cloned.1.call-done = f32[4096,128]{1,0:T(8,128)} async-done(((f32[1024,128]{1,0:T(8,128)}), f32[4096,128]{1,0:T(8,128)}) %all-gather.10.cloned.1.call-update) | async-done | bytes 2097168 | tf_op jit(solution)/shard_map/all_gather | solution.py:24
  124.8 4.0 gather_fusion.2
  128.8 8.1 %convolution_multiply_fusion.5 = f32[48,128,128]{2,1,0:T(8,128)} fusion(f32[48,128,128]{2,1,0:T(8,128)} %gather_fusion.2, f32[48,128,128]{2,1,0:T(8,128)S(1)} %copy-done, f32[48]{0:T(128)S(1)} %convert_element_type.14), kind=kOutput, calls=%fused_computation.19 | convolution fusion | flops 1208745984 | bytes 9437376 | tf_op jit(solution)/shard_map/sij,sjk->sik/dot_general | solution.py:26
  136.9 2.9 reduce_sum.64
  139.9 2.0 copy.28
  144.7 2.2 fusion.27
  147.8 11.1 %all_gather.47 = f32[1024,128]{1,0:T(8,128)} all-gather(f32[128,128]{1,0:T(8,128)S(1)} %slice_multiply_fusion.4), channel_id=1, replica_groups=mesh['dom'=8,'near'=4] {'dom'}, dimensions={0}, use_global_device_ids=true | all-gather | bytes 589824 | tf_op jit(solution)/shard_map/all_gather | solution.py:31
  158.9 2.4 gather_fusion.5
  161.4 30.3 %all-gather.12.cloned.1.call-done = f32[4096,128]{1,0:T(8,128)} async-done(((f32[1024,128]{1,0:T(8,128)}), f32[4096,128]{1,0:T(8,128)}) %all-gather.12.cloned.1.call-update) | async-done | bytes 2097168 | tf_op jit(solution)/shard_map/all_gather | solution.py:24
  191.7 4.0 gather_fusion.4
  195.7 8.1 %convolution_multiply_fusion.4 = f32[48,128,128]{2,1,0:T(8,128)} fusion(f32[48,128,128]{2,1,0:T(8,128)} %gather_fusion.4, f32[48,128,128]{2,1,0:T(8,128)S(1)} %copy-done, f32[48]{0:T(128)S(1)} %convert_element_type.14), kind=kOutput, calls=%fused_computation.18 | convolution fusion | flops 1208745984 | bytes 9437376 | tf_op jit(solution)/shard_map/sij,sjk->sik/dot_general | solution.py:26
  203.8 2.9 reduce_sum.65
  206.7 2.0 copy.30
  210.7 2.4 fusion.24
  213.1 2.8 fusion.44
  217.5 11.4 %all_gather.49 = f32[1024,128]{1,0:T(8,128)} all-gather(f32[128,128]{1,0:T(8,128)S(1)} %slice_multiply_fusion.3), channel_id=1, replica_groups=mesh['dom'=8,'near'=4] {'dom'}, dimensions={0}, use_global_device_ids=true | all-gather | bytes 589824 | tf_op jit(solution)/shard_map/all_gather | solution.py:31
  228.9 2.4 gather_fusion.7
  231.3 101.0 %all-reduce.4.cloned.1.call-done = f32[128,128]{0,1:T(8,128)} async-done(((f32[128,128]{0,1:T(8,128)}), f32[128,128]{0,1:T(8,128)}) %all-reduce.4.cloned.1.call-update) | async-done | bytes 65552 | tf_op jit(solution)/shard_map/psum | solution.py:89
  334.1 11.7 %cholesky.44 = f32[128,128]{1,0:T(8,128)S(1)} custom-call(f32[128,128]{1,0:T(8,128)S(1)} %fusion.39), custom_call_target="Cholesky" | custom-call | tf_op jit(solution)/shard_map/jit(cholesky)/cholesky | solution.py:64
  347.2 9.8 %custom-call.6 = f32[1,128,128]{1,2,0:T(8,128)S(1)} custom-call(f32[1,128,128]{2,1,0:T(8,128)S(1)} %fusion.34), custom_call_target="InvertDiagBlocksLowerTriangular" | custom-call | tf_op jit(solution)/shard_map/jit(_solve_triangular)/triangular_solve | solution.py:65
  357.3 2.5 fusion.45
  359.8 21.2 %all-gather.14.cloned.1.call-done = f32[4096,128]{1,0:T(8,128)} async-done(((f32[1024,128]{1,0:T(8,128)}), f32[4096,128]{1,0:T(8,128)}) %all-gather.14.cloned.1.call-update) | async-done | bytes 2097168 | tf_op jit(solution)/shard_map/all_gather | solution.py:24
  381.0 4.0 gather_fusion.6
  385.0 8.3 %convolution_multiply_fusion.3 = f32[48,128,128]{2,1,0:T(8,128)} fusion(f32[48,128,128]{2,1,0:T(8,128)} %gather_fusion.6, f32[48,128,128]{2,1,0:T(8,128)S(1)} %copy-done, f32[48]{0:T(128)S(1)} %convert_element_type.14), kind=kOutput, calls=%fused_computation.17 | convolution fusion | flops 1208745984 | bytes 9437376 | tf_op jit(solution)/shard_map/sij,sjk->sik/dot_general | solution.py:26
  393.3 2.9 reduce_sum.66
  396.2 2.1 copy.32
  403.9 11.2 %all_gather.51 = f32[1024,128]{1,0:T(8,128)} all-gather(f32[128,128]{1,0:T(8,128)S(1)} %slice_multiply_fusion.2), channel_id=1, replica_groups=mesh['dom'=8,'near'=4] {'dom'}, dimensions={0}, use_global_device_ids=true | all-gather | bytes 589824 | tf_op jit(solution)/shard_map/all_gather | solution.py:31
  415.1 2.4 gather_fusion.9
  417.5 30.8 %all-gather.16.cloned.1.call-done = f32[4096,128]{1,0:T(8,128)} async-done(((f32[1024,128]{1,0:T(8,128)}), f32[4096,128]{1,0:T(8,128)}) %all-gather.16.cloned.1.call-update) | async-done | bytes 2097168 | tf_op jit(solution)/shard_map/all_gather | solution.py:24
  448.3 4.0 gather_fusion.8
  452.3 8.1 %convolution_multiply_fusion.2 = f32[48,128,128]{2,1,0:T(8,128)} fusion(f32[48,128,128]{2,1,0:T(8,128)} %gather_fusion.8, f32[48,128,128]{2,1,0:T(8,128)S(1)} %copy-done, f32[48]{0:T(128)S(1)} %convert_element_type.14), kind=kOutput, calls=%fused_computation.16 | convolution fusion | flops 1208745984 | bytes 9437376 | tf_op jit(solution)/shard_map/sij,sjk->sik/dot_general | solution.py:26
  460.4 2.9 reduce_sum.67
  463.3 2.0 copy.36
  467.3 2.1 fusion.21
  470.5 10.8 %all_gather.53 = f32[1024,128]{1,0:T(8,128)} all-gather(f32[128,128]{1,0:T(8,128)S(1)} %slice_multiply_fusion.1), channel_id=1, replica_groups=mesh['dom'=8,'near'=4] {'dom'}, dimensions={0}, use_global_device_ids=true | all-gather | bytes 589824 | tf_op jit(solution)/shard_map/all_gather | solution.py:31
  481.3 2.4 gather_fusion.11
  483.7 30.6 %all-gather.18.cloned.1.call-done = f32[4096,128]{1,0:T(8,128)} async-done(((f32[1024,128]{1,0:T(8,128)}), f32[4096,128]{1,0:T(8,128)}) %all-gather.18.cloned.1.call-update) | async-done | bytes 2097168 | tf_op jit(solution)/shard_map/all_gather | solution.py:24
  514.3 4.0 gather_fusion.10
  518.3 8.3 %convolution_multiply_fusion.1 = f32[48,128,128]{2,1,0:T(8,128)} fusion(f32[48,128,128]{2,1,0:T(8,128)} %gather_fusion.10, f32[48,128,128]{2,1,0:T(8,128)S(1)} %copy-done, f32[48]{0:T(128)S(1)} %convert_element_type.14), kind=kOutput, calls=%fused_computation.15 | convolution fusion | flops 1208745984 | bytes 9437376 | tf_op jit(solution)/shard_map/sij,sjk->sik/dot_general | solution.py:26
  526.6 2.9 reduce_sum.68
  529.5 2.1 copy.38
  533.5 2.1 fusion.18
  536.7 10.8 %all_gather.55 = f32[1024,128]{1,0:T(8,128)} all-gather(f32[128,128]{1,0:T(8,128)S(1)} %slice_multiply_fusion), channel_id=1, replica_groups=mesh['dom'=8,'near'=4] {'dom'}, dimensions={0}, use_global_device_ids=true | all-gather | bytes 589824 | tf_op jit(solution)/shard_map/all_gather | solution.py:31
  547.5 2.4 gather_fusion.13
  549.9 3.0 fusion.46
  552.9 27.6 %all-gather.20.cloned.1.call-done = f32[4096,128]{1,0:T(8,128)} async-done(((f32[1024,128]{1,0:T(8,128)}), f32[4096,128]{1,0:T(8,128)}) %all-gather.20.cloned.1.call-update) | async-done | bytes 2097168 | tf_op jit(solution)/shard_map/all_gather | solution.py:24
  580.5 4.0 gather_fusion.12
  584.5 8.3 %convolution_multiply_fusion = f32[48,128,128]{2,1,0:T(8,128)} fusion(f32[48,128,128]{2,1,0:T(8,128)} %gather_fusion.12, f32[48,128,128]{2,1,0:T(8,128)S(1)} %copy-done, f32[48]{0:T(128)S(1)} %convert_element_type.14), kind=kOutput, calls=%fused_computation.14 | convolution fusion | flops 1208745984 | bytes 9437376 | tf_op jit(solution)/shard_map/sij,sjk->sik/dot_general | solution.py:26
  592.8 2.9 reduce_sum.69
  595.8 2.0 copy.42
  599.8 3.0 fusion.14
  602.8 121.6 %all-reduce.6.cloned.1.call-done = (f32[128,128]{0,1:T(8,128)}, f32[128,128]{0,1:T(8,128)}) async-done(((f32[128,128]{0,1:T(8,128)}, f32[128,128]{0,1:T(8,128)}), (f32[128,128]{0,1:T(8,128)}, f32[128,128]{0,1:T(8,128)})) %all-reduce.6.cloned.1.call-update) | async-done | bytes 131088 | tf_op jit(solution)/shard_map/psum | solution.py:89
  726.2 11.7 %cholesky.55 = f32[128,128]{1,0:T(8,128)S(1)} custom-call(f32[128,128]{1,0:T(8,128)S(1)} %fusion.37), custom_call_target="Cholesky" | custom-call | tf_op jit(solution)/shard_map/jit(cholesky)/cholesky | solution.py:64
  739.2 9.8 %custom-call.7 = f32[1,128,128]{1,2,0:T(8,128)S(1)} custom-call(f32[1,128,128]{2,1,0:T(8,128)S(1)} %fusion.35), custom_call_target="InvertDiagBlocksLowerTriangular" | custom-call | tf_op jit(solution)/shard_map/jit(_solve_triangular)/triangular_solve | solution.py:65
  749.3 2.4 fusion.47
  (66 shorter events, 39.7 us)
Async XLA Ops:
  7.2 55.1 %copy-start = (f32[48,128,128]{2,1,0:T(8,128)S(1)}, f32[48,128,128]{2,1,0:T(8,128)}, u32[]{:S(2)}) copy-start(f32[48,128,128]{2,1,0:T(8,128)} %param.12) | copy-start | bytes 9437188
  7.2 51.1 %all-gather.8.cloned.1.call-start = ((), (), s32[]{:S(2)}) async-start(), calls=%async_computation | async-start | bytes 2621440 | tf_op jit(solution)/shard_map/all_gather | solution.py:24
  7.9 116.9 %all-gather.10.cloned.1.call-start = ((), (), s32[]{:S(2)}) async-start(), calls=%async_computation.1 | async-start | bytes 2621440 | tf_op jit(solution)/shard_map/all_gather | solution.py:24
  77.3 0.8 copy-start.1
  80.0 111.6 %all-gather.12.cloned.1.call-start = ((), (), s32[]{:S(2)}) async-start(), calls=%async_computation.2 | async-start | bytes 2621440 | tf_op jit(solution)/shard_map/all_gather | solution.py:24
  143.9 0.8 copy-start.2
  146.9 185.5 %all-reduce.4.cloned.1.call-start = ((), (), s32[]{:S(2)}) async-start(), calls=%async_computation.4 | async-start | bytes 131072 | tf_op jit(solution)/shard_map/psum | solution.py:89
  216.0 165.0 %all-gather.14.cloned.1.call-start = ((), (), s32[]{:S(2)}) async-start(), calls=%async_computation.3 | async-start | bytes 2621440 | tf_op jit(solution)/shard_map/all_gather | solution.py:24
  216.6 231.7 %all-gather.16.cloned.1.call-start = ((), (), s32[]{:S(2)}) async-start(), calls=%async_computation.5 | async-start | bytes 2621440 | tf_op jit(solution)/shard_map/all_gather | solution.py:24
  398.2 3.1 copy-start.3
  402.9 111.4 %all-gather.18.cloned.1.call-start = ((), (), s32[]{:S(2)}) async-start(), calls=%async_computation.6 | async-start | bytes 2621440 | tf_op jit(solution)/shard_map/all_gather | solution.py:24
  469.5 111.0 %all-gather.20.cloned.1.call-start = ((), (), s32[]{:S(2)}) async-start(), calls=%async_computation.7 | async-start | bytes 2621440 | tf_op jit(solution)/shard_map/all_gather | solution.py:24
  535.7 188.7 %all-reduce.6.cloned.1.call-start = ((), (), s32[]{:S(2)}) async-start(), calls=%async_computation.8 | async-start | bytes 262144 | tf_op jit(solution)/shard_map/psum | solution.py:89
Sparse Core Ops, SparseCore 0:
  9.6 48.6 all-gather.7
  80.1 44.6 all-gather.9
  147.0 44.6 all-gather.11
  216.1 116.2 all-reduce.3
  334.3 46.6 all-gather.13
  403.1 45.2 all-gather.15
  469.6 44.6 all-gather.17
  535.8 44.6 all-gather.19
  602.9 121.4 all-reduce.5
where the time goes:
time: 771 us; the launch traced here: 761 us
  waiting for transfers between devices  426 us (55%)
  other arithmetic  90.6 us (12%)
  matrix products  88.9 us (12%)
  blocking collectives  78.5 us (10%)
  local copies, waits for them, and re-layouts  61.1 us (8%)
  between operations  15.2 us (2%)
    psum x2, waiting for transfers between devices, local(): lax.psum((inner(filtered, filtered), inner(filtered, filtered_image)), ('...  223 us
    all_gather x7, waiting for transfers between devices, apply_operator(): gathered = lax.all_gather(block, 'near', axis=0, tiled=True)  202 us
    all_gather x7, blocking collectives, apply_operator(): lax.all_gather(edge_tile, 'dom', axis=0, tiled=True)  78.5 us
    dot_general x7, matrix products, apply_operator(): jnp.einsum('sij,sjk->sik', near_tiles, picked, precision=lax.Precision.HI...  57.3 us
    gather x7, local copies, waits for them, and re-layouts, apply_operator(): gathered.reshape(group_size * tiles_dev, tile_rows, width)[near_src]  28 us
    another operation x6, other arithmetic, inverse_factor(): lower = jnp.linalg.cholesky(gram)  24.8 us
    another operation x4, other arithmetic, inverse_factor(): jax.scipy.linalg.solve_triangular(lower, jnp.eye(gram.shape[0], dtype=jnp...  20.9 us
    reduce_sum x7, other arithmetic, apply_operator(): near_sum = products.reshape(tiles_dev, NPER, tile_rows, width).sum(axis=1)  20.4 us
  transfers between devices with their start and end apart: 9, of which 9 were waited for; matrix products, arithmetic and copies ran while one was open for 7% of the time, Pallas kernels for 0%

commit v1 on v0

v1 whole, which is shorter than its diff:
```python
from functools import partial

import jax
import jax.numpy as jnp
from jax import lax
from jax.experimental import pallas as pl
from jax.experimental.pallas import tpu as pltpu
from jax.sharding import PartitionSpec as P

NPER = 6
NBT = 4
ITERS = 2
DEG = 3
LOWER_EDGE = 0.6
UPPER_EDGE = 2.0
CENTER = (UPPER_EDGE + LOWER_EDGE) / 2.0
HALF = (UPPER_EDGE - LOWER_EDGE) / 2.0
OPS = ITERS * DEG + 1
MESH = pl.DeviceIdType.MESH
HIGHEST = lax.Precision.HIGHEST
F32 = jnp.float32
BF16 = jnp.bfloat16


def split(value, axis):
    high = value.astype(BF16)
    low = (value - high.astype(F32)).astype(BF16)
    return jnp.concatenate([high, low], axis=axis)


def quadrants(total):
    rows, columns = total.shape[0] // 2, total.shape[1] // 2
    return (total[:rows, :columns] + total[rows:, :columns]) + (
        total[:rows, columns:] + total[rows:, columns:]
    )


def inner(left, right):
    total = lax.dot_general(
        split(left, 1), split(right, 1), (((0,), (0,)), ((), ())), preferred_element_type=F32
    )
    return quadrants(total)


def times_transposed(block, factor):
    return lax.dot_general(
        block, factor, (((1,), (1,)), ((), ())), precision=HIGHEST, preferred_element_type=F32
    )


def factor_steps(gram, out_ref, per_yield):
    size = gram.shape[0]
    rows = lax.broadcasted_iota(jnp.int32, (size, size), 0)
    lanes = lax.broadcasted_iota(jnp.int32, (size, size), 1)
    right = jnp.where(rows == lanes, 1.0, 0.0).astype(F32)
    left = gram
    base = 0
    for j in range(size):
        if j - base == 8:
            left, right = left[8:], right[8:]
            base = j
        at = j - base
        row = left[at : at + 1, :]
        root = lax.rsqrt(row[:, j : j + 1])
        row_right = right[at : at + 1, :] * root
        column = left[:, j : j + 1] * root
        out_ref[j : j + 1, :] = row_right
        if j < size - 1:
            left = left - column * (row * root)
            right = right - column * row_right
        if (j + 1) % per_yield == 0:
            yield


def kernel(
    n_dom,
    n_near,
    start_ref,
    near_ref,
    src_ref,
    mask_ref,
    far_ref,
    far_src_ref,
    far_mask_ref,
    count_ref,
    enc_ref,
    ray_ref,
    *scratch,
):
    group = scratch[:OPS]
    edge = scratch[OPS : 2 * OPS]
    (
        staged,
        weights,
        image,
        inverse_1,
        inverse_2,
        parts_out,
        parts_in,
        planes,
        gathered,
        near_recv,
        near_send,
        edge_recv,
        edge_send,
        red_in_recv,
        red_in_send,
        red_plane_recv,
        red_plane_send,
        red_out_recv,
        red_out_send,
        load_sem,
    ) = scratch[2 * OPS :]
    tiles = start_ref.shape[0]
    tile_rows, width = start_ref.shape[1], start_ref.shape[2]
    nodes_all = tiles * tile_rows * n_dom * n_near
    dom = lax.axis_index("dom")
    near = lax.axis_index("near")
    mine = near * tiles
    slices = parts_out.shape[1]
    slice_rows = parts_out.shape[2]

    loads = [
        pltpu.make_async_copy(near_ref, staged.at[pl.ds(0, tiles * NPER)], load_sem.at[0]),
        pltpu.make_async_copy(far_ref, staged.at[pl.ds(tiles * NPER, tiles)], load_sem.at[1]),
    ]
    for load in loads:
        load.start()

    barrier = pltpu.get_barrier_semaphore()
    for i in range(1, n_dom):
        pl.semaphore_signal(
            barrier, inc=1, device_id={"dom": lax.rem(dom + i, n_dom)}, device_id_type=MESH
        )
    for i in range(1, n_near):
        pl.semaphore_signal(
            barrier, inc=1, device_id={"near": lax.rem(near + i, n_near)}, device_id_type=MESH
        )
    pl.semaphore_wait(barrier, n_dom + n_near - 2)

    def near_copy(k, owner, t, step):
        place = group[k].at[owner * tiles + t]
        way = 0 if step < 0 else 1
        return pltpu.make_async_remote_copy(
            src_ref=place,
            dst_ref=place,
            send_sem=near_send.at[k % 2, way, owner * NBT + t],
            recv_sem=near_recv.at[k, owner * NBT + t],
            device_id={"near": near + step},
            device_id_type=MESH,
        )

    def send_near(k, owner, t):
        @pl.when(near < n_near - 1)
        def _():
            near_copy(k, owner, t, 1).start()

        @pl.when(near > 0)
        def _():
            near_copy(k, owner, t, -1).start()

    def edge_copy(k, i):
        place = edge[k].at[dom]
        return pltpu.make_async_remote_copy(
            src_ref=place,
            dst_ref=place,
            send_sem=edge_send.at[k % 2, i],
            recv_sem=edge_recv.at[k, dom],
            device_id={"dom": lax.rem(dom + i, n_dom)},
            device_id_type=MESH,
        )

    def send_edge(k, tile):
        rows = lax.broadcasted_iota(jnp.int32, tile.shape, 0)
        edge[k][dom] = jnp.where(rows < count_ref[0], tile, 0.0)

        @pl.loop(1, n_dom)
        def _(i):
            edge_copy(k, i).start()

    def put(k, r, tile):
        group[k][mine + r] = tile

    def exchange(k, background):
        for d in range(1, n_near):
            for t in range(NBT):

                @pl.when(near >= d)
                def _():
                    owner = near - d
                    near_copy(k, owner, t, -1).wait_recv()

                    @pl.when(near < n_near - 1)
                    def _():
                        near_copy(k, owner, t, 1).start()

                @pl.when(near + d < n_near)
                def _():
                    owner = near + d
                    near_copy(k, owner, t, 1).wait_recv()

                    @pl.when(near > 0)
                    def _():
                        near_copy(k, owner, t, -1).start()

                next(background, None)
        for _ in background:
            pass

        @pl.loop(1, n_dom)
        def _(i):
            owner = lax.rem(dom + i, n_dom)
            place = edge[k].at[owner]
            pltpu.make_async_remote_copy(
                src_ref=place,
                dst_ref=place,
                send_sem=edge_send.at[k % 2, i],
                recv_sem=edge_recv.at[k, owner],
                device_id={"dom": owner},
                device_id_type=MESH,
            ).wait_recv()

    def finish_sends(k):
        for owner in range(n_near):

            @pl.when((near >= owner) & (near < n_near - 1))
            def _():
                @pl.loop(0, NBT)
                def _(t):
                    near_copy(k, owner, t, 1).wait_send()

            @pl.when((near <= owner) & (near > 0))
            def _():
                @pl.loop(0, NBT)
                def _(t):
                    near_copy(k, owner, t, -1).wait_send()

        @pl.loop(1, n_dom)
        def _(i):
            edge_copy(k, i).wait_send()

    def apply_row(k, r):
        picked = [group[k][src_ref[r * NPER + s]] for s in range(NPER)]
        picked.append(edge[k][far_src_ref[r]])
        right = jnp.concatenate([split(tile, 1) for tile in picked], axis=0)
        total = jnp.dot(weights[r], right, preferred_element_type=F32)
        return group[k][mine + r] - quadrants(total)

    def advance(k, r):
        present = group[k][mine + r]
        moved = (apply_row(k, r) - CENTER * present) / HALF
        if k % DEG == 0:
            return moved
        return 2.0 * moved - group[k - 1][mine + r]

    def reduce_steps(at, value):
        for j in range(slices):
            parts_out[at, j] = value[j * slice_rows : (j + 1) * slice_rows]

        def owner_only(body):
            if slices == n_dom:
                body()
            else:
                pl.when(dom < slices)(body)

        def in_copy(i, owner):
            peer = lax.rem(dom + i, n_dom)
            return pltpu.make_async_remote_copy(
                src_ref=parts_out.at[at, lax.rem(peer, slices)],
                dst_ref=parts_in.at[at, owner],
                send_sem=red_in_send.at[at, i],
                recv_sem=red_in_recv.at[at, owner],
                device_id={"dom": peer},
                device_id_type=MESH,
            )

        def to_owner(i, body):
            if slices == n_dom:
                body()
            else:
                pl.when(lax.rem(dom + i, n_dom) < slices)(body)

        def plane_copy(i, owner):
            return pltpu.make_async_remote_copy(
                src_ref=planes.at[at, owner],
                dst_ref=planes.at[at, owner],
                send_sem=red_plane_send.at[at, i],
                recv_sem=red_plane_recv.at[at, owner],
                device_id={"near": lax.rem(near + i, n_near)},
                device_id_type=MESH,
            )

        def out_copy(i, owner):
            return pltpu.make_async_remote_copy(
                src_ref=gathered.at[at, owner],
                dst_ref=gathered.at[at, owner],
                send_sem=red_out_send.at[at, i],
                recv_sem=red_out_recv.at[at, owner],
                device_id={"dom": lax.rem(dom + i, n_dom)},
                device_id_type=MESH,
            )

        for i in range(1, n_dom):
            to_owner(i, lambda: in_copy(i, dom).start())
        yield

        def near_sum():
            parts_in[at, dom] = parts_out[at, lax.rem(dom, slices)]
            for i in range(1, n_dom):
                in_copy(i, lax.rem(dom + i, n_dom)).wait_recv()
            planes[at, near] = jnp.sum(parts_in[at], axis=0)
            for i in range(1, n_near):
                plane_copy(i, near).start()

        owner_only(near_sum)
        yield

        def all_sum():
            for i in range(1, n_near):
                plane_copy(i, lax.rem(near + i, n_near)).wait_recv()
            gathered[at, dom] = jnp.sum(planes[at], axis=0)
            for i in range(1, n_dom):
                out_copy(i, dom).start()

        owner_only(all_sum)
        yield
        for i in range(1, n_dom):
            owner = lax.rem(dom + i, n_dom)
            to_owner(i, lambda: out_copy(i, owner).wait_recv())
            to_owner(i, lambda: in_copy(i, dom).wait_send())
            owner_only(lambda: out_copy(i, dom).wait_send())
        for i in range(1, n_near):
            owner_only(lambda: plane_copy(i, near).wait_send())
        yield

    def reduced(at):
        return jnp.concatenate([gathered[at, j] for j in range(slices)], axis=0) * (1.0 / nodes_all)

    def own_block(k):
        first = pl.multiple_of(mine, tiles)
        return group[k][pl.ds(first, tiles)].reshape(tiles * tile_rows, width)

    def prepare_steps():
        for load in loads:
            load.wait()

        @pl.loop(0, tiles)
        def _(r):
            for s in range(NPER + 1):
                if s < NPER:
                    tile = staged[r * NPER + s] * mask_ref[r * NPER + s].astype(F32)
                else:
                    tile = staged[tiles * NPER + r] * far_mask_ref[r].astype(F32)
                weights[r, :, s * tile_rows : (s + 1) * tile_rows] = split(tile, 0)

        yield

    def background(k):
        if k == 0:
            yield from prepare_steps()
        if k == DEG:
            block = own_block(k)
            yield
            steps = reduce_steps(0, inner(block, block))
            for _ in steps:
                yield
                yield
        if k == DEG + 1:
            yield from factor_steps(reduced(0), inverse_1, 12)
        if k == OPS - 1:
            block = own_block(k)
            steps = reduce_steps(1, inner(block, block))
            for _ in steps:
                yield
                yield
            yield from factor_steps(reduced(1), inverse_2, 32)

    for r in range(tiles):
        put(0, r, start_ref[r])
        if r < NBT:
            send_near(0, mine // tiles, r)
        if r == 0:
            send_edge(0, start_ref[0])

    for k in range(OPS):
        exchange(k, background(k))
        if k > 0:
            finish_sends(k - 1)
        if k < OPS - 1:

            def step(r):
                tile = advance(k, r)
                if k == OPS - 2:
                    tile = times_transposed(tile, inverse_1[...])
                put(k + 1, r, tile)
                return tile

            send_edge(k + 1, step(0))
            send_near(k + 1, near, 0)

            @pl.loop(1, NBT)
            def _(r):
                step(r)
                send_near(k + 1, near, r)

            @pl.loop(NBT, tiles)
            def _(r):
                step(r)

        else:

            @pl.loop(0, tiles)
            def _(r):
                image[r] = apply_row(k, r)

    finish_sends(OPS - 1)
    last = own_block(OPS - 1)
    steps = reduce_steps(2, inner(last, image[...].reshape(tiles * tile_rows, width)))
    next(steps)
    lower_inverse = inverse_2[...]

    @pl.loop(0, tiles)
    def _(r):
        enc_ref[r] = times_transposed(group[OPS - 1][mine + r], inverse_2[...])

    for _ in steps:
        pass
    ray_ref[...] = times_transposed(
        jnp.dot(lower_inverse, reduced(2), precision=HIGHEST, preferred_element_type=F32),
        lower_inverse,
    )


def local(
    n_dom,
    n_near,
    start_block,
    near_tiles,
    near_src,
    near_mask,
    far_tiles,
    far_src,
    far_mask,
    bound_count,
):
    tile_rows = near_tiles.shape[1]
    width = start_block.shape[1]
    tiles = start_block.shape[0] // tile_rows
    slices = min(n_dom, width // 8)
    slice_rows = width // slices
    vmem = pl.BlockSpec(memory_space=pltpu.VMEM)
    smem = pl.BlockSpec(memory_space=pltpu.SMEM)
    hbm = pl.BlockSpec(memory_space=pl.ANY)
    dma = pltpu.SemaphoreType.DMA
    scratch = [pltpu.VMEM((n_near * tiles, tile_rows, width), F32) for _ in range(OPS)]
    scratch += [pltpu.VMEM((n_dom, tile_rows, width), F32) for _ in range(OPS)]
    scratch += [
        pltpu.VMEM((tiles * (NPER + 1), tile_rows, tile_rows), F32),
        pltpu.VMEM((tiles, 2 * tile_rows, (NPER + 1) * tile_rows), BF16),
        pltpu.VMEM((tiles, tile_rows, width), F32),
        pltpu.VMEM((width, width), F32),
        pltpu.VMEM((width, width), F32),
        pltpu.VMEM((3, slices, slice_rows, width), F32),
        pltpu.VMEM((3, n_dom, slice_rows, width), F32),
        pltpu.VMEM((3, n_near, slice_rows, width), F32),
        pltpu.VMEM((3, n_dom, slice_rows, width), F32),
        dma((OPS, n_near * NBT)),
        dma((2, 2, n_near * NBT)),
        dma((OPS, n_dom)),
        dma((2, n_dom)),
        dma((3, n_dom)),
        dma((3, n_dom)),
        dma((3, n_near)),
        dma((3, n_near)),
        dma((3, n_dom)),
        dma((3, n_dom)),
        dma((2,)),
    ]
    enc, ray = pl.pallas_call(
        partial(kernel, n_dom, n_near),
        out_shape=(
            jax.ShapeDtypeStruct((tiles, tile_rows, width), F32),
            jax.ShapeDtypeStruct((width, width), F32),
        ),
        in_specs=[vmem, hbm, smem, smem, hbm, smem, smem, smem],
        out_specs=(vmem, vmem),
        scratch_shapes=scratch,
        compiler_params=pltpu.CompilerParams(
            collective_id=0, has_side_effects=True, vmem_limit_bytes=60 * 1024 * 1024
        ),
    )(
        start_block.reshape(tiles, tile_rows, width),
        near_tiles,
        near_src,
        near_mask,
        far_tiles,
        far_src,
        far_mask,
        bound_count,
    )
    return enc.reshape(start_block.shape), ray


def solution(mesh):
    shape = dict(mesh.shape)
    rows = ("dom", "near")
    return jax.shard_map(
        partial(local, shape["dom"], shape["near"]),
        mesh=mesh,
        in_specs=(
            P(rows, None),
            P(rows, None, None),
            P(rows),
            P(rows),
            P(rows, None, None),
            P(rows),
            P(rows),
            P(rows),
        ),
        out_specs=(P(rows, None), P()),
        check_vma=False,
    )
```

time: 771 us -> 162 us (0.21); the launches traced: 761 us -> 161 us
  waiting for transfers between devices: 426 us -> 0 us
  Pallas kernels: 0 us -> 157 us
  other arithmetic: 90.6 us -> 0 us
  matrix products: 88.9 us -> 0 us
  blocking collectives: 78.5 us -> 0 us
  local copies, waits for them, and re-layouts: 61.1 us -> 3.34 us
  between operations: 15.2 us -> 1.29 us
    psum x2 -> x0, waiting for transfers between devices: 223 us -> none  [local(): lax.psum((inner(filtered, filtered), inner(filtered, filtered_image)), ('...]
    all_gather x7 -> x0, waiting for transfers between devices: 202 us -> none  [apply_operator(): gathered = lax.all_gather(block, 'near', axis=0, tiled=True)]
    pallas_call x0 -> x1, Pallas kernels: none -> 157 us  [local(): pl.pallas_call(partial(kernel, n_dom, n_near), out_shape=(jax.ShapeDtypeS...]
    dot_general x22 -> x0, matrix products: 88.3 us -> none  [the longest x7 57.3 us: apply_operator(): jnp.einsum('sij,sjk->sik', near_tiles, picked, precision=lax.Precision.HI...]
    all_gather x7 -> x0, blocking collectives: 78.5 us -> none  [apply_operator(): lax.all_gather(edge_tile, 'dom', axis=0, tiled=True)]
    another operation x10 -> x0, other arithmetic: 45.7 us -> none  [the longest x6 24.8 us: inverse_factor(): lower = jnp.linalg.cholesky(gram)]
    gather x14 -> x0, local copies, waits for them, and re-layouts: 45 us -> none  [the longest x7 28 us: apply_operator(): gathered.reshape(group_size * tiles_dev, tile_rows, width)[near_src]]
    reduce_sum x7 -> x0, other arithmetic: 20.4 us -> none  [apply_operator(): near_sum = products.reshape(tiles_dev, NPER, tile_rows, width).sum(axis=1)]
  transfers between devices with their start and end apart: 9 -> 0, of which waited for: 9 -> 0; matrix products, arithmetic and copies ran while one was open for 7% -> 0% of each run, Pallas kernels for 0% -> 0%
where the time goes in v1:
time: 162 us; the launch traced here: 161 us
  Pallas kernels  157 us (97%)
  local copies, waits for them, and re-layouts  3.34 us (2%)
    pallas_call x1, Pallas kernels, local(): pl.pallas_call(partial(kernel, n_dom, n_near), out_shape=(jax.ShapeDtypeS...  157 us
    unnamed x2, local copies, waits for them, and re-layouts  3.34 us

profile of v1, /device:TPU:0, one launch (start us, length us, event | category | flops | bytes accessed | tf_op | source)
XLA Modules:
  0.0 161.3 jit_solution(1982929087180179657)
XLA Ops:
  1.3 156.7 %shard_map.95 = (f32[8,128,128]{2,1,0:T(8,128)}, f32[128,128]{1,0:T(8,128)}) custom-call(f32[8,128,128]{2,1,0:T(8,128)} %bitcast.3, f32[48,128,128]{2,1,0:T(8,128)} %near_ref.1, s32[48]{0:T(128)} %src_ref.1, s32[48]{0:T(128)} %mask_ref.1, f32[8,128,128]{2,1,0:T(8,128)} %far_ref.1, s32[8]{0:T(128)} %far_src_ref.1, s32[8]{0:T(128)} %far_mask_ref.1, ...), custom_call_target="tpu_custom_call" | custom-call | tf_op jit(solution)/shard_map/pallas_call | solution.py:479
  157.9 1.9 %copy.13 = f32[1024,128]{1,0:T(8,128)} copy(f32[1024,128]{1,0:T(8,128)} %bitcast.2) | data formatting | bytes 1048576
  159.8 1.5 copy.14

commit v2 on v1

--- a/solution.py
+++ b/solution.py
@@ -181,31 +181,48 @@
     def put(k, r, tile):
         group[k][mine + r] = tile
 
-    def exchange(k, background):
+    def forward(k, owner, t):
+        @pl.when((owner < near) & (near < n_near - 1))
+        def _():
+            near_copy(k, owner, t, -1).wait_recv()
+            near_copy(k, owner, t, 1).start()
+
+        @pl.when((owner > near) & (near > 0))
+        def _():
+            near_copy(k, owner, t, 1).wait_recv()
+            near_copy(k, owner, t, -1).start()
+
+    def exchange(k, hooks):
+        pairs = (n_near + 1) // 2
+        upper = near >= n_near // 2
         for d in range(1, n_near):
             for t in range(NBT):
 
                 @pl.when(near >= d)
                 def _():
-                    owner = near - d
-                    near_copy(k, owner, t, -1).wait_recv()
-
-                    @pl.when(near < n_near - 1)
-                    def _():
-                        near_copy(k, owner, t, 1).start()
+                    forward(k, near - d, t)
 
                 @pl.when(near + d < n_near)
                 def _():
-                    owner = near + d
-                    near_copy(k, owner, t, 1).wait_recv()
-
-                    @pl.when(near > 0)
-                    def _():
-                        near_copy(k, owner, t, -1).start()
-
-                next(background, None)
-        for _ in background:
-            pass
+                    forward(k, near + d, t)
+
+                if d == 2 and t == 1:
+                    hooks["late"]()
+            if d == 1:
+                hooks["middle"]()
+        hooks["end"]()
+
+        @pl.when(near == 0)
+        def _():
+            @pl.loop(NBT, n_near * NBT)
+            def _(i):
+                near_copy(k, i // NBT, lax.rem(i, NBT), 1).wait_recv()
+
+        @pl.when(near == n_near - 1)
+        def _():
+            @pl.loop(0, (n_near - 1) * NBT)
+            def _(i):
+                near_copy(k, i // NBT, lax.rem(i, NBT), -1).wait_recv()
 
         @pl.loop(1, n_dom)
         def _(i):
@@ -340,7 +357,7 @@
         first = pl.multiple_of(mine, tiles)
         return group[k][pl.ds(first, tiles)].reshape(tiles * tile_rows, width)
 
-    def prepare_steps():
+    def prepare():
         for load in loads:
             load.wait()
 
@@ -353,27 +370,37 @@
                     tile = staged[tiles * NPER + r] * far_mask_ref[r].astype(F32)
                 weights[r, :, s * tile_rows : (s + 1) * tile_rows] = split(tile, 0)
 
-        yield
-
-    def background(k):
+    running = {}
+
+    def go_on(name):
+        return lambda: next(running[name], None)
+
+    def begin_reduce(at, k):
+        block = own_block(k)
+        running[at] = reduce_steps(at, inner(block, block))
+        next(running[at])
+
+    def begin_factor(at, out_ref, per_yield):
+        next(running[at])
+        running["factor"] = factor_steps(reduced(at), out_ref, per_yield)
+        next(running["factor"])
+
+    def hooks_of(k):
+        hooks = {name: lambda: None for name in ("middle", "late", "end")}
+        if k == DEG or k == OPS - 1:
+            at = 0 if k == DEG else 1
+            begin_reduce(at, k)
+            hooks["middle"] = go_on(at)
+            hooks["late"] = go_on(at)
         if k == 0:
-            yield from prepare_steps()
-        if k == DEG:
-            block = own_block(k)
-            yield
-            steps = reduce_steps(0, inner(block, block))
-            for _ in steps:
-                yield
-                yield
+            hooks["middle"] = prepare
         if k == DEG + 1:
-            yield from factor_steps(reduced(0), inverse_1, 12)
+            hooks["end"] = lambda: begin_factor(0, inverse_1, width // 2)
+        if k == DEG + 2:
+            hooks["end"] = go_on("factor")
         if k == OPS - 1:
-            block = own_block(k)
-            steps = reduce_steps(1, inner(block, block))
-            for _ in steps:
-                yield
-                yield
-            yield from factor_steps(reduced(1), inverse_2, 32)
+            hooks["end"] = lambda: begin_factor(1, inverse_2, width)
+        return hooks
 
     for r in range(tiles):
         put(0, r, start_ref[r])
@@ -383,7 +410,7 @@
             send_edge(0, start_ref[0])
 
     for k in range(OPS):
-        exchange(k, background(k))
+        exchange(k, hooks_of(k))
         if k > 0:
             finish_sends(k - 1)
         if k < OPS - 1:

time: 162 us -> 159 us (0.981)
  Pallas kernels: 157 us -> 154 us
    pallas_call x1, Pallas kernels: 157 us -> 154 us  [local(): pl.pallas_call(partial(kernel, n_dom, n_near), out_shape=(jax.ShapeDtypeS...]
where the time goes in v2:
time: 159 us
  Pallas kernels  154 us (97%)
  local copies, waits for them, and re-layouts  3.34 us (2%)
    pallas_call x1, Pallas kernels, local(): pl.pallas_call(partial(kernel, n_dom, n_near), out_shape=(jax.ShapeDtypeS...  154 us
    unnamed x2, local copies, waits for them, and re-layouts  3.34 us

profile of v2, /device:TPU:0, one launch (start us, length us, event | category | flops | bytes accessed | tf_op | source)
XLA Modules:
  0.0 159.1 jit_solution(11191368964503123994)
XLA Ops:
  1.3 154.4 %shard_map.95 = (f32[8,128,128]{2,1,0:T(8,128)}, f32[128,128]{1,0:T(8,128)}) custom-call(f32[8,128,128]{2,1,0:T(8,128)} %bitcast.3, f32[48,128,128]{2,1,0:T(8,128)} %near_ref.1, s32[48]{0:T(128)} %src_ref.1, s32[48]{0:T(128)} %mask_ref.1, f32[8,128,128]{2,1,0:T(8,128)} %far_ref.1, s32[8]{0:T(128)} %far_src_ref.1, s32[8]{0:T(128)} %far_mask_ref.1, ...), custom_call_target="tpu_custom_call" | custom-call | tf_op jit(solution)/shard_map/pallas_call | solution.py:506
  155.7 1.9 %copy.13 = f32[1024,128]{1,0:T(8,128)} copy(f32[1024,128]{1,0:T(8,128)} %bitcast.2) | data formatting | bytes 1048576
  157.6 1.5 copy.14
